TPU v7x, 512 devices: a whole 4x8x8 slice. The times are simulated.
512 devices in a mesh: seq: 16 (over y, core), wide: 32 (over z, x).
Axes of the slice: x: 4, y: 8, z: 8, core: 2. Of those that a mesh axis runs over, the one named last changes fastest.
Arguments:
- out_gate: bfloat16 [65536, 4096], P(('seq', 'wide')), may hold values from -6 to 6
- in_gate: bfloat16 [65536, 4096], P(('seq', 'wide')), may hold values from -6 to 6
- values: bfloat16 [65536, 4096], P(('seq', 'wide')), may hold values from -6 to 6
- filter_taps: bfloat16 [4096, 4096], P('seq', 'wide'), may hold values from -0.09375 to 0.09375
- skip_gain: float32 [4096], P('wide'), may hold values from 0.5 to 1.5
Outputs:
- mixed: bfloat16 [65536, 4096], P(('seq', 'wide'))
All inputs are finite; a program needn't handle non-finite values.
Results may differ from a plain program's by a relative error of at most 0.0065.
Values may be sent and summed in bfloat16 or wider, within the bound.
A program may use at most 64 MiB of HBM per device.

v0:
```python
import math
import jax
import jax.numpy as jnp
from jax import lax
from jax.sharding import PartitionSpec as P

PRECISE = lax.Precision.HIGH


def passed_along(value, axis, by):
    length = lax.axis_size(axis)
    pairs = [(i, i + by) for i in range(length) if 0 <= i + by < length]
    return lax.ppermute(value, axis, pairs)


def phase_table(first_count, second_count, modulus):
    first_index = lax.iota(jnp.int32, first_count)
    second_index = lax.iota(jnp.int32, second_count)
    product = first_index[:, None] * second_index[None, :] % modulus
    angle_table = product.astype(jnp.float32) * (-2.0 * math.pi / modulus)
    return (jnp.cos(angle_table), jnp.sin(angle_table))


def column_block(column_count, orientation):
    cosine_table, sine_table = phase_table(column_count, column_count, column_count)
    upper_rows = jnp.stack([cosine_table, orientation * sine_table], axis=1)
    bottom = jnp.stack([-orientation * sine_table, cosine_table], axis=1)
    return jnp.stack([upper_rows, bottom], axis=0)


def rotate(pair_parts, row_count, column_count, padded_size, orientation):
    twist_cosine, twist_sine = phase_table(row_count, column_count, padded_size)
    twist_sine = orientation * twist_sine
    real_part = pair_parts[0] * twist_cosine[:, :, None] - pair_parts[1] * twist_sine[:, :, None]
    imaginary = pair_parts[0] * twist_sine[:, :, None] + pair_parts[1] * twist_cosine[:, :, None]
    return jnp.stack([real_part, imaginary], axis=0)


def causal_filter(signal, tap_columns, padded_size):
    column_count = 64
    channels = signal.shape[1]
    rows_used = max(signal.shape[0], tap_columns.shape[0]) // column_count
    row_count = padded_size // column_count
    half_rows = row_count // 2 + 1
    cosine_first, sine_first = phase_table(row_count, rows_used, row_count)
    first_table = jnp.concatenate(
        [
            jnp.concatenate([cosine_first, -sine_first], axis=1),
            jnp.concatenate([sine_first, cosine_first], axis=1),
        ],
        axis=0,
    )
    joined = jnp.concatenate(
        [
            signal.reshape(rows_used, column_count * channels),
            tap_columns.reshape(rows_used, column_count * channels),
        ],
        axis=0,
    )
    first = jnp.dot(first_table, joined, precision=PRECISE).reshape(
        2, row_count, column_count, channels
    )
    turned = rotate(first, row_count, column_count, padded_size, 1.0)
    spectrum = jnp.einsum(
        "panc,pnqk->qakc", turned, column_block(column_count, 1.0), precision=PRECISE
    )
    kept = spectrum[:, :half_rows]
    zero_row = jnp.roll(jnp.flip(spectrum[:, :1], axis=2), 1, axis=2)
    mirrored = jnp.flip(spectrum[:, row_count // 2 :], axis=(1, 2))
    partner = jnp.concatenate([zero_row, mirrored], axis=1)
    signal_real = 0.5 * (kept[0] + partner[0])
    signal_imag = 0.5 * (kept[1] - partner[1])
    taps_real = 0.5 * (kept[1] + partner[1])
    taps_imag = 0.5 * (partner[0] - kept[0])
    product_real = signal_real * taps_real - signal_imag * taps_imag
    product_imag = signal_real * taps_imag + signal_imag * taps_real
    product = jnp.stack([product_real, product_imag], axis=0)
    mixed = jnp.einsum(
        "pakc,pkqn->qanc", product, column_block(column_count, -1.0), precision=PRECISE
    )
    returned = rotate(mixed, half_rows, column_count, padded_size, -1.0)
    cosine_last, sine_last = phase_table(row_count, half_rows, row_count)
    frequency = lax.iota(jnp.int32, half_rows)
    weights = jnp.where((frequency == 0) | (frequency == row_count // 2), 1.0, 2.0).astype(
        jnp.float32
    )
    last_table = (
        jnp.concatenate([cosine_last * weights[None, :], sine_last * weights[None, :]], axis=1)
        / padded_size
    )
    flattened = returned.reshape(2 * half_rows, column_count * channels)
    result = jnp.dot(last_table, flattened, precision=PRECISE)
    return result.reshape(padded_size, channels)


def local(out_gate, in_gate, values, filter_taps, skip_gain):
    gated_values = (in_gate.astype(jnp.float32) * values.astype(jnp.float32)).astype(jnp.bfloat16)
    all_taps = lax.all_gather(filter_taps, "seq", axis=0, tiled=True)
    by_channel = lax.all_to_all(gated_values, "wide", split_axis=1, concat_axis=0, tiled=True)
    group_length = by_channel.shape[0]
    tap_count = all_taps.shape[0]
    linear = causal_filter(by_channel, all_taps, group_length + tap_count)
    own_part = linear[:group_length]
    future = linear[group_length:]
    incoming = passed_along(future.astype(jnp.bfloat16), "seq", 1).astype(future.dtype)
    convolved = own_part + incoming
    filtered = (convolved + skip_gain[None, :] * by_channel.astype(jnp.float32)).astype(
        jnp.bfloat16
    )
    returned = lax.all_to_all(filtered, "wide", split_axis=0, concat_axis=1, tiled=True)
    return (out_gate.astype(jnp.float32) * returned.astype(jnp.float32)).astype(jnp.bfloat16)


def solution(mesh):
    in_specs = (
        P(("seq", "wide"), None),
        P(("seq", "wide"), None),
        P(("seq", "wide"), None),
        P("seq", "wide"),
        P("wide"),
    )
    out_specs = P(("seq", "wide"), None)
    return jax.shard_map(local, mesh=mesh, in_specs=in_specs, out_specs=out_specs, check_vma=False)
```

profile of v0, /device:TPU:18, one launch (start us, length us, event | category | flops | bytes accessed | tf_op | source)
XLA Modules:
  0.0 184.0 jit_solution(17083957285483094685)
XLA Ops:
  6.5 1.6 copy.25
  8.2 1.6 copy.26
  11.4 13.5 %all-to-all-start = ((bf16[128,32,128]{2,0,1:T(8,128)(2,1)}), bf16[128,32,128]{2,0,1:T(8,128)(2,1)S(1)}, u32[]{:S(2)}, u32[]{:S(2)}) async-start(bf16[128,32,128]{2,0,1:T(8,128)(2,1)} %copy.27), calls=%async_computation | async-start | bytes 2097152 | tf_op jit(solution)/shard_map/all_to_all | solution.py:99
  29.1 39.1 %all-gather.2.cloned.1.call-done = bf16[4096,128]{1,0:T(8,128)(2,1)} async-done(((bf16[256,128]{1,0:T(8,128)(2,1)}), bf16[4096,128]{1,0:T(8,128)(2,1)}) %all-gather.2.cloned.1.call-update) | async-done | bytes 1048592 | tf_op jit(solution)/shard_map/all_gather | solution.py:98
  70.2 3.4 %fusion.16 = f32[256,8192]{1,0:T(8,128)S(1)} fusion(bf16[64,8192]{1,0:T(8,128)(2,1)S(1)} %reshape.233, bf16[64,8192]{1,0:T(8,128)(2,1)S(1)} %reshape.232, f32[128,64]{1,0:T(8,128)} %get-tuple-element.22, f32[128,64]{1,0:T(8,128)S(1)} %get-tuple-element.21, f32[128,64]{1,0:T(8,128)S(1)} %fusion.74), kind=kOutput, calls=%fused_computation.31 | convolution fusion | flops 1614905344 | bytes 10584064 | tf_op jit(solution)/shard_map/dot_general | solution.py:60
  76.0 2.5 %fusion.8 = (f32[1,128,64,128]{3,2,0,1:T(8,128)S(1)}, f32[1,128,64,128]{3,2,0,1:T(8,128)S(1)}) fusion(f32[128,64]{1,0:T(8,128)S(1)} %get-tuple-element.23, f32[128,64]{1,0:T(8,128)S(1)} %get-tuple-element.24, f32[1,128,64,128]{3,2,1,0:T(8,128)S(1)} %bitcast.110, f32[1,128,64,128]{3,2,1,0:T(8,128)S(1)} %bitcast.111), kind=kLoop, calls=%fused_computation.13 | loop fusion | flops 6291456 | bytes 16842752 | tf_op jit(solution)/shard_map/sub | solution.py:34
  78.5 4.3 %fusion.12 = f32[2,128,64,128]{3,2,1,0:T(8,128)S(1)} fusion(f32[1,128,64,128]{3,2,0,1:T(8,128)S(1)} %get-tuple-element.8, f32[1,128,64,128]{3,2,0,1:T(8,128)S(1)} %get-tuple-element.7, f32[1,64,2,64]{1,3,0,2:T(8,128)S(1)} %copy-done.6, f32[1,64,2,64]{1,3,0,2:T(8,128)S(1)} %copy-done.7), kind=kOutput, calls=%fused_computation.20 | convolution fusion | flops 1612726272 | bytes 16842752 | tf_op jit(solution)/shard_map/panc,pnqk->qakc/dot_general | solution.py:64
  82.9 2.8 %slice.86 = f32[2,64,64,128]{3,2,1,0:T(8,128)} slice(f32[2,128,64,128]{3,2,1,0:T(8,128)S(1)} %fusion.12), slice={[0:2], [64:128], [0:64], [0:128]} | slice | bytes 8388608 | tf_op jit(solution)/shard_map/slice | solution.py:69
  85.7 1.7 copy-done
  87.4 6.6 %rev.6 = f32[2,64,64,128]{3,2,1,0:T(8,128)} reverse(f32[2,64,64,128]{3,2,1,0:T(8,128)} %slice.86), dimensions={1,2} | reverse | bytes 8388608 | tf_op jit(solution)/shard_map/jit(_flip)/rev | solution.py:69
  94.0 2.9 %pad_maximum_fusion = f32[2,65,64,128]{3,2,1,0:T(8,128)S(1)} fusion(f32[2,64,64,128]{3,2,1,0:T(8,128)} %rev.6, f32[2,1,63,128]{3,2,1,0:T(8,128)S(1)} %slice.71, f32[2,1,1,128]{3,2,1,0:T(1,128)S(1)} %slice.84), kind=kLoop, calls=%fused_computation.4 | loop fusion | flops 2129920 | bytes 8519680 | tf_op jit(solution)/shard_map/concatenate | solution.py:70
  96.9 1.7 copy-done.1
  98.7 1.5 multiply_subtract_fusion.1
  100.3 2.2 %fusion.13 = f32[2,65,64,128]{3,2,1,0:T(8,128)S(1)} fusion(f32[1,65,64,128]{3,2,1,0:T(8,128)S(1)} %get-tuple-element.6, f32[1,65,64,128]{3,2,1,0:T(8,128)S(1)} %get-tuple-element.5, f32[1,64,2,64]{1,3,2,0:T(8,128)S(1)} %copy-done.5, f32[1,64,2,64]{1,3,2,0:T(8,128)S(1)} %copy-done.4), kind=kOutput, calls=%fused_computation.21 | convolution fusion | flops 818970624 | bytes 8585216 | tf_op jit(solution)/shard_map/pakc,pkqn->qanc/dot_general | solution.py:78
  104.9 3.6 %copy.44 = f32[17,8,64,128]{3,1,2,0:T(8,128)S(1)} copy(f32[17,8,64,128]{3,2,1,0:T(8,128)S(1)} %bitcast.108) | data formatting | bytes 8912896
  108.4 2.1 %fusion.23 = f32[128,8192]{1,0:T(8,128)S(1)} fusion(f32[130,8192]{1,0:T(8,128)S(1)} %bitcast.107, f32[128,65]{1,0:T(8,128)S(1)} %get-tuple-element.20, f32[128,65]{1,0:T(8,128)S(1)} %get-tuple-element.19), kind=kOutput, calls=%fused_computation.42 | convolution fusion | flops 817922560 | bytes 8520704 | tf_op jit(solution)/shard_map/dot_general | solution.py:92
  110.6 1.9 %copy-done.2 = f32[128,8192]{1,0:T(8,128)} copy-done((f32[128,8192]{1,0:T(8,128)}, f32[128,8192]{1,0:T(8,128)S(1)}, u32[]{:S(2)}) %copy-start.2) | copy-done | bytes 4194328
  113.6 2.5 %convert_element_type.128 = bf16[4096,128]{1,0:T(8,128)(2,1)} reshape(bf16[64,8192]{1,0:T(8,128)(2,1)} %slice.141) | data formatting | bytes 2097152 | tf_op jit(solution)/shard_map/convert_element_type | solution.py:105
  116.1 2.3 %collective-permute-start = (bf16[4096,128]{1,0:T(8,128)(2,1)}, bf16[4096,128]{1,0:T(8,128)(2,1)}, u32[]{:S(2)}, u32[]{:S(2)}) collective-permute-start(bf16[4096,128]{1,0:T(8,128)(2,1)} %convert_element_type.128), channel_id=1, source_target_pairs={{0,32},{32,64},{64,96},{96,128},{128,160},{160,192},{192,224},{224... | collective-permute-start | bytes 3145736 | tf_op jit(solution)/shard_map/ppermute | solution.py:13
  118.4 1.5 slice.79
  119.9 12.7 %collective-permute-done = bf16[4096,128]{1,0:T(8,128)(2,1)} collective-permute-done((bf16[4096,128]{1,0:T(8,128)(2,1)}, bf16[4096,128]{1,0:T(8,128)(2,1)}, u32[]{:S(2)}, u32[]{:S(2)}) %collective-permute-start) | collective-permute-done | bytes 1048608 | tf_op jit(solution)/shard_map/ppermute | solution.py:13
  132.7 3.2 %fusion.22 = bf16[4096,128]{1,0:T(8,128)(2,1)} fusion(f32[4096,128]{1,0:T(8,128)} %slice.79, bf16[4096,128]{1,0:T(8,128)(2,1)} %collective-permute-done, bf16[128,32,128]{2,0,1:T(8,128)(2,1)S(1)} %all-to-all-done, f32[128]{0:T(128)S(1)} %copy-done.10), kind=kLoop, calls=%fused_computation.39 | loop fusion | flops 3145728 | bytes 5243392 | tf_op jit(solution)/shard_map/convert_element_type | solution.py:107
  135.9 10.6 %all-to-all-start.1 = ((bf16[32,128,128]{2,1,0:T(8,128)(2,1)}), bf16[32,128,128]{2,1,0:T(8,128)(2,1)S(1)}, u32[]{:S(2)}, u32[]{:S(2)}) async-start(bf16[32,128,128]{2,1,0:T(8,128)(2,1)} %bitcast.25), calls=%async_computation.1 | async-start | bytes 2097152 | tf_op jit(solution)/shard_map/all_to_all | solution.py:110
  147.2 27.7 %all-to-all-done.1 = bf16[32,128,128]{2,1,0:T(8,128)(2,1)S(1)} async-done(((bf16[32,128,128]{2,1,0:T(8,128)(2,1)}), bf16[32,128,128]{2,1,0:T(8,128)(2,1)S(1)}, u32[]{:S(2)}, u32[]{:S(2)}) %all-to-all-start.1) | async-done | bytes 1048608 | tf_op jit(solution)/shard_map/all_to_all | solution.py:110
  (51 shorter events, 16.6 us)
Async XLA Ops:
  11.4 58.4 %all-to-all-start = ((bf16[128,32,128]{2,0,1:T(8,128)(2,1)}), bf16[128,32,128]{2,0,1:T(8,128)(2,1)S(1)}, u32[]{:S(2)}, u32[]{:S(2)}) async-start(bf16[128,32,128]{2,0,1:T(8,128)(2,1)} %copy.27), calls=%async_computation | async-start | bytes 2097152 | tf_op jit(solution)/shard_map/all_to_all | solution.py:99
  24.8 43.4 %all-gather.2.cloned.1.call-start = ((), (), s32[]{:S(2)}) async-start(), calls=%async_computation.2 | async-start | bytes 1114112 | tf_op jit(solution)/shard_map/all_gather | solution.py:98
  76.0 2.5 %copy-start.6 = (f32[1,64,2,64]{1,3,0,2:T(8,128)S(1)}, f32[1,64,2,64]{1,3,0,2:T(8,128)}, u32[]{:S(2)}) copy-start(f32[1,64,2,64]{1,3,0,2:T(8,128)} %get-tuple-element.14) | copy-start | bytes 98308
  76.0 2.5 %copy-start.7 = (f32[1,64,2,64]{1,3,0,2:T(8,128)S(1)}, f32[1,64,2,64]{1,3,0,2:T(8,128)}, u32[]{:S(2)}) copy-start(f32[1,64,2,64]{1,3,0,2:T(8,128)} %get-tuple-element.17) | copy-start | bytes 98308
  82.9 4.5 %copy-start = (f32[2,128,64,128]{3,2,1,0:T(8,128)}, f32[2,128,64,128]{3,2,1,0:T(8,128)S(1)}, u32[]{:S(2)}) copy-start(f32[2,128,64,128]{3,2,1,0:T(8,128)S(1)} %fusion.12) | copy-start | bytes 25165828
  94.0 4.6 %copy-start.1 = (f32[2,128,64,128]{3,2,1,0:T(8,128)S(1)}, f32[2,128,64,128]{3,2,1,0:T(8,128)}, u32[]{:S(2)}) copy-start(f32[2,128,64,128]{3,2,1,0:T(8,128)} %copy-done) | copy-start | bytes 25165828
  98.7 1.5 copy-start.4
  98.7 1.5 copy-start.5
  100.2 2.2 %copy-start.8 = (f32[65,64]{1,0:T(8,128)S(1)}, f32[65,64]{1,0:T(8,128)}, u32[]{:S(2)}) copy-start(f32[65,64]{1,0:T(8,128)} %get-tuple-element.27) | copy-start | bytes 49924
  100.2 2.2 %copy-start.9 = (f32[65,64]{1,0:T(8,128)S(1)}, f32[65,64]{1,0:T(8,128)}, u32[]{:S(2)}) copy-start(f32[65,64]{1,0:T(8,128)} %get-tuple-element.28) | copy-start | bytes 49924
  110.6 2.0 %copy-start.2 = (f32[128,8192]{1,0:T(8,128)}, f32[128,8192]{1,0:T(8,128)S(1)}, u32[]{:S(2)}) copy-start(f32[128,8192]{1,0:T(8,128)S(1)} %fusion.23) | copy-start | bytes 12582916
  113.6 4.8 %slice-start = ((f32[128,8192]{1,0:T(8,128)}), f32[64,8192]{1,0:T(8,128)S(1)}, s32[]{:S(2)}) async-start(f32[128,8192]{1,0:T(8,128)} %copy-done.2), calls=%async_computation.3 | async-start | bytes 4194304 | tf_op jit(solution)/shard_map/slice | solution.py:103
  116.1 16.6 %copy-start.10 = (f32[128]{0:T(128)S(1)}, f32[128]{0:T(128)}, u32[]{:S(2)}) copy-start(f32[128]{0:T(128)} %param.9) | copy-start | bytes 1540
  116.1 16.6 %collective-permute-start = (bf16[4096,128]{1,0:T(8,128)(2,1)}, bf16[4096,128]{1,0:T(8,128)(2,1)}, u32[]{:S(2)}, u32[]{:S(2)}) collective-permute-start(bf16[4096,128]{1,0:T(8,128)(2,1)} %convert_element_type.128), channel_id=1, source_target_pairs={{0,32},{32,64},{64,96},{96,128},{128,160},{160,192},{192,224},{224... | collective-permute-start | bytes 3145736 | tf_op jit(solution)/shard_map/ppermute | solution.py:13
  119.9 26.6 %copy-start.3 = (bf16[128,4096]{1,0:T(8,128)(2,1)S(1)}, bf16[128,4096]{1,0:T(8,128)(2,1)}, u32[]{:S(2)}) copy-start(bf16[128,4096]{1,0:T(8,128)(2,1)} %param.5) | copy-start | bytes 3145732
  135.9 39.0 %all-to-all-start.1 = ((bf16[32,128,128]{2,1,0:T(8,128)(2,1)}), bf16[32,128,128]{2,1,0:T(8,128)(2,1)S(1)}, u32[]{:S(2)}, u32[]{:S(2)}) async-start(bf16[32,128,128]{2,1,0:T(8,128)(2,1)} %bitcast.25), calls=%async_computation.1 | async-start | bytes 2097152 | tf_op jit(solution)/shard_map/all_to_all | solution.py:110
Sparse Core Ops, SparseCore 0:
  27.8 40.3 all-gather.1
where the time goes:
time: 185 us; the launch traced here: 184 us
  waiting for transfers between devices  80.2 us (43%)
  local copies, waits for them, and re-layouts  35.4 us (19%)
  starting transfers between devices  26.3 us (14%)
  other arithmetic  16.2 us (9%)
  between operations  13.8 us (7%)
  matrix products  12 us (6%)
    all_gather x1, waiting for transfers between devices, local(): all_taps = lax.all_gather(filter_taps, 'seq', axis=0, tiled=True)  39.1 us
    all_to_all x1, waiting for transfers between devices, local(): lax.all_to_all(filtered, 'wide', split_axis=0, concat_axis=1, tiled=True)  27.7 us
    unnamed x30, local copies, waits for them, and re-layouts  15.6 us
    all_to_all x1, starting transfers between devices, local(): lax.all_to_all(gated_values, 'wide', split_axis=1, concat_axis=0, tiled=T...  13.5 us
    ppermute x1, waiting for transfers between devices, passed_along(): return lax.ppermute(value, axis, pairs)  12.7 us
    all_to_all x1, starting transfers between devices, local(): lax.all_to_all(filtered, 'wide', split_axis=0, concat_axis=1, tiled=True)  10.6 us
    rev x1, local copies, waits for them, and re-layouts, causal_filter(): mirrored = jnp.flip(spectrum[:, row_count // 2:], axis=(1, 2))  6.63 us
    dot_general x1, matrix products, causal_filter(): jnp.einsum('panc,pnqk->qakc', turned, column_block(column_count, 1.0), pr...  4.32 us
  transfers between devices with their start and end apart: 4, of which 3 were waited for; matrix products, arithmetic and copies ran while one was open for 4% of the time, Pallas kernels for 0%

commit v1 on v0

--- a/solution.py
+++ b/solution.py
@@ -5,6 +5,13 @@
 from jax.sharding import PartitionSpec as P
 
 PRECISE = lax.Precision.HIGH
+
+
+def list_digits_here(message, dim_i):
+    message = jnp.moveaxis(message, 0, dim_i)
+    extra = message.shape
+    big = message.reshape(*extra[:dim_i], extra[dim_i] * extra[dim_i + 1], *extra[dim_i + 2 :])
+    return big
 
 
 def passed_along(value, axis, by):
@@ -95,7 +102,19 @@
 
 def local(out_gate, in_gate, values, filter_taps, skip_gain):
     gated_values = (in_gate.astype(jnp.float32) * values.astype(jnp.float32)).astype(jnp.bfloat16)
-    all_taps = lax.all_gather(filter_taps, "seq", axis=0, tiled=True)
+    devs = lax.axis_size("seq")
+    chunks = [(k0, (k0 + 1) % devs) for k0 in range(devs)]
+    upper, built = ([], [])
+    made = [(src_i, to_i) for to_i, src_i in chunks]
+    for nth in range(devs - 1):
+        if nth % 2 == 0:
+            upper.append(lax.ppermute(upper[-1] if upper else filter_taps, "seq", chunks))
+        else:
+            built.append(lax.ppermute(built[-1] if built else filter_taps, "seq", made))
+    row_out = jnp.stack([*upper[::-1], filter_taps, *built])
+    mixed_arr = lax.axis_index("seq") - len(upper)
+    row_out = row_out[(jnp.arange(devs) - mixed_arr) % devs]
+    all_taps = list_digits_here(row_out, 0)
     by_channel = lax.all_to_all(gated_values, "wide", split_axis=1, concat_axis=0, tiled=True)
     group_length = by_channel.shape[0]
     tap_count = all_taps.shape[0]

time: 185 us -> 166 us (0.90)
  the two profiles are of different devices: /device:TPU:18 before, /device:TPU:27 now
where the time goes in v1:
time: 166 us; the launch traced here: 165 us
  starting transfers between devices  53.9 us (32%)
  waiting for transfers between devices  44.5 us (27%)
  local copies, waits for them, and re-layouts  37.9 us (23%)
  other arithmetic  16.7 us (10%)
  matrix products  11.9 us (7%)
    ppermute x8, starting transfers between devices, local(): lax.ppermute(upper[-1] if upper else filter_taps, 'seq', chunks)  28 us
    all_to_all x1, waiting for transfers between devices, local(): lax.all_to_all(filtered, 'wide', split_axis=0, concat_axis=1, tiled=True)  25.8 us
    unnamed x47, local copies, waits for them, and re-layouts  18.3 us
    all_to_all x1, starting transfers between devices, local(): lax.all_to_all(gated_values, 'wide', split_axis=1, concat_axis=0, tiled=T...  12.9 us
    ppermute x1, waiting for transfers between devices, passed_along(): return lax.ppermute(value, axis, pairs)  10.5 us
    all_to_all x1, starting transfers between devices, local(): lax.all_to_all(filtered, 'wide', split_axis=0, concat_axis=1, tiled=True)  9.21 us
    rev x1, local copies, waits for them, and re-layouts, causal_filter(): mirrored = jnp.flip(spectrum[:, row_count // 2:], axis=(1, 2))  6.62 us
    ppermute x7, waiting for transfers between devices, local(): built.append(lax.ppermute(built[-1] if built else filter_taps, 'seq', made))  5.09 us
  transfers between devices with their start and end apart: 18, of which 15 were waited for; matrix products, arithmetic and copies ran while one was open for 9% of the time, Pallas kernels for 0%

profile of v1, /device:TPU:27, one launch (start us, length us, event | category | flops | bytes accessed | tf_op | source)
XLA Modules:
  0.0 165.4 jit_solution(18382404725582557566)
XLA Ops:
  0.0 3.1 %collective-permute-start = (bf16[256,128]{1,0:T(8,128)(2,1)}, bf16[256,128]{1,0:T(8,128)(2,1)S(1)}, u32[]{:S(2)}, u32[]{:S(2)}) collective-permute-start(bf16[256,128]{1,0:T(8,128)(2,1)} %param.8), channel_id=1, source_target_pairs={{0,32},{32,64},{64,96},{96,128},{128,160},{160,192},{192,224},{224... | collective-permute-start | bytes 196616 | tf_op jit(solution)/shard_map/ppermute | solution.py:111
  7.9 12.9 %all-to-all-start = ((bf16[128,32,128]{2,0,1:T(8,128)(2,1)}), bf16[128,32,128]{2,0,1:T(8,128)(2,1)S(1)}, u32[]{:S(2)}, u32[]{:S(2)}) async-start(bf16[128,32,128]{2,0,1:T(8,128)(2,1)} %copy.27), calls=%async_computation | async-start | bytes 2097152 | tf_op jit(solution)/shard_map/all_to_all | solution.py:118
  21.4 3.5 %collective-permute-start.1 = (bf16[256,128]{1,0:T(8,128)(2,1)S(1)}, bf16[256,128]{1,0:T(8,128)(2,1)S(1)}, u32[]{:S(2)}, u32[]{:S(2)}) collective-permute-start(bf16[256,128]{1,0:T(8,128)(2,1)S(1)} %collective-permute-done), channel_id=1, source_target_pairs={{0,32},{32,64},{64,96},{96,128},{128,160},{160,192},{192,224},{224... | collective-permute-start | bytes 196616 | tf_op jit(solution)/shard_map/ppermute | solution.py:111
  26.3 3.6 %collective-permute-start.2 = (bf16[256,128]{1,0:T(8,128)(2,1)S(1)}, bf16[256,128]{1,0:T(8,128)(2,1)S(1)}, u32[]{:S(2)}, u32[]{:S(2)}) collective-permute-start(bf16[256,128]{1,0:T(8,128)(2,1)S(1)} %collective-permute-done.1), channel_id=1, source_target_pairs={{0,32},{32,64},{64,96},{96,128},{128,160},{160,192},{192,224},{224... | collective-permute-start | bytes 196616 | tf_op jit(solution)/shard_map/ppermute | solution.py:111
  31.2 3.6 %collective-permute-start.3 = (bf16[256,128]{1,0:T(8,128)(2,1)S(1)}, bf16[256,128]{1,0:T(8,128)(2,1)S(1)}, u32[]{:S(2)}, u32[]{:S(2)}) collective-permute-start(bf16[256,128]{1,0:T(8,128)(2,1)S(1)} %collective-permute-done.2), channel_id=1, source_target_pairs={{0,32},{32,64},{64,96},{96,128},{128,160},{160,192},{192,224},{224... | collective-permute-start | bytes 196616 | tf_op jit(solution)/shard_map/ppermute | solution.py:111
  36.1 3.6 %collective-permute-start.4 = (bf16[256,128]{1,0:T(8,128)(2,1)S(1)}, bf16[256,128]{1,0:T(8,128)(2,1)S(1)}, u32[]{:S(2)}, u32[]{:S(2)}) collective-permute-start(bf16[256,128]{1,0:T(8,128)(2,1)S(1)} %collective-permute-done.3), channel_id=1, source_target_pairs={{0,32},{32,64},{64,96},{96,128},{128,160},{160,192},{192,224},{224... | collective-permute-start | bytes 196616 | tf_op jit(solution)/shard_map/ppermute | solution.py:111
  41.0 3.6 %collective-permute-start.5 = (bf16[256,128]{1,0:T(8,128)(2,1)S(1)}, bf16[256,128]{1,0:T(8,128)(2,1)S(1)}, u32[]{:S(2)}, u32[]{:S(2)}) collective-permute-start(bf16[256,128]{1,0:T(8,128)(2,1)S(1)} %collective-permute-done.4), channel_id=1, source_target_pairs={{0,32},{32,64},{64,96},{96,128},{128,160},{160,192},{192,224},{224... | collective-permute-start | bytes 196616 | tf_op jit(solution)/shard_map/ppermute | solution.py:111
  45.9 3.6 %collective-permute-start.6 = (bf16[256,128]{1,0:T(8,128)(2,1)S(1)}, bf16[256,128]{1,0:T(8,128)(2,1)S(1)}, u32[]{:S(2)}, u32[]{:S(2)}) collective-permute-start(bf16[256,128]{1,0:T(8,128)(2,1)S(1)} %collective-permute-done.5), channel_id=1, source_target_pairs={{0,32},{32,64},{64,96},{96,128},{128,160},{160,192},{192,224},{224... | collective-permute-start | bytes 196616 | tf_op jit(solution)/shard_map/ppermute | solution.py:111
  50.8 3.6 %collective-permute-start.7 = (bf16[256,128]{1,0:T(8,128)(2,1)S(1)}, bf16[256,128]{1,0:T(8,128)(2,1)S(1)}, u32[]{:S(2)}, u32[]{:S(2)}) collective-permute-start(bf16[256,128]{1,0:T(8,128)(2,1)S(1)} %collective-permute-done.6), channel_id=1, source_target_pairs={{0,32},{32,64},{64,96},{96,128},{128,160},{160,192},{192,224},{224... | collective-permute-start | bytes 196616 | tf_op jit(solution)/shard_map/ppermute | solution.py:111
  62.2 3.3 %fusion.16 = f32[256,8192]{1,0:T(8,128)S(1)} fusion(bf16[64,8192]{1,0:T(8,128)(2,1)S(1)} %reshape_reshape.3, bf16[64,8192]{1,0:T(8,128)(2,1)S(1)} %reshape.278, f32[128,64]{1,0:T(8,128)S(1)} %get-tuple-element.22, f32[128,64]{1,0:T(8,128)S(1)} %get-tuple-element.21, f32[128,64]{1,0:T(8,128)} %fusion.74), kind=kOutput, calls=%fused_computation.32 | convolution fusion | flops 1614905344 | bytes 10584064 | tf_op jit(solution)/shard_map/dot_general | solution.py:67
  67.9 2.6 %fusion.8 = (f32[1,128,64,128]{3,2,0,1:T(8,128)S(1)}, f32[1,128,64,128]{3,2,0,1:T(8,128)S(1)}) fusion(f32[128,64]{1,0:T(8,128)S(1)} %get-tuple-element.23, f32[128,64]{1,0:T(8,128)S(1)} %get-tuple-element.24, f32[1,128,64,128]{3,2,1,0:T(8,128)S(1)} %bitcast.144, f32[1,128,64,128]{3,2,1,0:T(8,128)S(1)} %bitcast.145), kind=kLoop, calls=%fused_computation.14 | loop fusion | flops 6291456 | bytes 16842752 | tf_op jit(solution)/shard_map/sub | solution.py:41
  70.6 4.3 %fusion.12 = f32[2,128,64,128]{3,2,1,0:T(8,128)S(1)} fusion(f32[1,128,64,128]{3,2,0,1:T(8,128)S(1)} %get-tuple-element.8, f32[1,128,64,128]{3,2,0,1:T(8,128)S(1)} %get-tuple-element.7, f32[1,64,2,64]{1,3,0,2:T(8,128)S(1)} %copy-done.6, f32[1,64,2,64]{1,3,0,2:T(8,128)S(1)} %copy-done.7), kind=kOutput, calls=%fused_computation.21 | convolution fusion | flops 1612726272 | bytes 16842752 | tf_op jit(solution)/shard_map/panc,pnqk->qakc/dot_general | solution.py:71
  74.9 2.8 %slice.88 = f32[2,64,64,128]{3,2,1,0:T(8,128)} slice(f32[2,128,64,128]{3,2,1,0:T(8,128)S(1)} %fusion.12), slice={[0:2], [64:128], [0:64], [0:128]} | slice | bytes 8388608 | tf_op jit(solution)/shard_map/slice | solution.py:76
  79.4 6.6 %rev.6 = f32[2,64,64,128]{3,2,1,0:T(8,128)} reverse(f32[2,64,64,128]{3,2,1,0:T(8,128)} %slice.88), dimensions={1,2} | reverse | bytes 8388608 | tf_op jit(solution)/shard_map/jit(_flip)/rev | solution.py:76
  86.1 2.9 %pad_maximum_fusion = f32[2,65,64,128]{3,2,1,0:T(8,128)S(1)} fusion(f32[2,64,64,128]{3,2,1,0:T(8,128)} %rev.6, f32[2,1,63,128]{3,2,1,0:T(8,128)S(1)} %slice.71, f32[2,1,1,128]{3,2,1,0:T(1,128)S(1)} %slice.86), kind=kLoop, calls=%fused_computation.5 | loop fusion | flops 2129920 | bytes 8519680 | tf_op jit(solution)/shard_map/concatenate | solution.py:77
  92.3 2.2 %fusion.13 = f32[2,65,64,128]{3,2,1,0:T(8,128)S(1)} fusion(f32[1,65,64,128]{3,2,1,0:T(8,128)S(1)} %get-tuple-element.6, f32[1,65,64,128]{3,2,1,0:T(8,128)S(1)} %get-tuple-element.5, f32[1,64,2,64]{1,3,2,0:T(8,128)S(1)} %copy-done.5, f32[1,64,2,64]{1,3,2,0:T(8,128)S(1)} %copy-done.4), kind=kOutput, calls=%fused_computation.22 | convolution fusion | flops 818970624 | bytes 8585216 | tf_op jit(solution)/shard_map/pakc,pkqn->qanc/dot_general | solution.py:85
  97.1 3.6 %copy.44 = f32[17,8,64,128]{3,1,2,0:T(8,128)S(1)} copy(f32[17,8,64,128]{3,2,1,0:T(8,128)S(1)} %bitcast.142) | data formatting | bytes 8912896
  100.7 2.1 %fusion.23 = f32[128,8192]{1,0:T(8,128)S(1)} fusion(f32[130,8192]{1,0:T(8,128)S(1)} %bitcast.141, f32[128,65]{1,0:T(8,128)S(1)} %get-tuple-element.20, f32[128,65]{1,0:T(8,128)S(1)} %get-tuple-element.19), kind=kOutput, calls=%fused_computation.43 | convolution fusion | flops 817922560 | bytes 8520704 | tf_op jit(solution)/shard_map/dot_general | solution.py:99
  105.9 2.5 %convert_element_type.128 = bf16[4096,128]{1,0:T(8,128)(2,1)} reshape(bf16[64,8192]{1,0:T(8,128)(2,1)} %slice.143) | data formatting | bytes 2097152 | tf_op jit(solution)/shard_map/convert_element_type | solution.py:124
  108.4 3.7 %collective-permute-start.15 = (bf16[4096,128]{1,0:T(8,128)(2,1)}, bf16[4096,128]{1,0:T(8,128)(2,1)}, u32[]{:S(2)}, u32[]{:S(2)}) collective-permute-start(bf16[4096,128]{1,0:T(8,128)(2,1)} %convert_element_type.128), channel_id=1, source_target_pairs={{0,32},{32,64},{64,96},{96,128},{128,160},{160,192},{192,224},{224... | collective-permute-start | bytes 3145736 | tf_op jit(solution)/shard_map/ppermute | solution.py:20
  113.7 10.5 %collective-permute-done.15 = bf16[4096,128]{1,0:T(8,128)(2,1)} collective-permute-done((bf16[4096,128]{1,0:T(8,128)(2,1)}, bf16[4096,128]{1,0:T(8,128)(2,1)}, u32[]{:S(2)}, u32[]{:S(2)}) %collective-permute-start.15) | collective-permute-done | bytes 1048608 | tf_op jit(solution)/shard_map/ppermute | solution.py:20
  124.2 3.2 %fusion.22 = bf16[4096,128]{1,0:T(8,128)(2,1)} fusion(f32[4096,128]{1,0:T(8,128)} %slice.79, bf16[4096,128]{1,0:T(8,128)(2,1)} %collective-permute-done.15, bf16[128,32,128]{2,0,1:T(8,128)(2,1)S(1)} %all-to-all-done, f32[128]{0:T(128)S(1)} %copy-done.11), kind=kLoop, calls=%fused_computation.40 | loop fusion | flops 3145728 | bytes 5243392 | tf_op jit(solution)/shard_map/convert_element_type | solution.py:126
  127.4 9.2 %all-to-all-start.1 = ((bf16[32,128,128]{2,1,0:T(8,128)(2,1)}), bf16[32,128,128]{2,1,0:T(8,128)(2,1)S(1)}, u32[]{:S(2)}, u32[]{:S(2)}) async-start(bf16[32,128,128]{2,1,0:T(8,128)(2,1)} %bitcast.42), calls=%async_computation.1 | async-start | bytes 2097152 | tf_op jit(solution)/shard_map/all_to_all | solution.py:129
  137.3 25.8 %all-to-all-done.1 = bf16[32,128,128]{2,1,0:T(8,128)(2,1)S(1)} async-done(((bf16[32,128,128]{2,1,0:T(8,128)(2,1)}), bf16[32,128,128]{2,1,0:T(8,128)(2,1)S(1)}, u32[]{:S(2)}, u32[]{:S(2)}) %all-to-all-start.1) | async-done | bytes 1048608 | tf_op jit(solution)/shard_map/all_to_all | solution.py:129
  (99 shorter events, 38.5 us)
Async XLA Ops:
  0.0 21.4 %collective-permute-start = (bf16[256,128]{1,0:T(8,128)(2,1)}, bf16[256,128]{1,0:T(8,128)(2,1)S(1)}, u32[]{:S(2)}, u32[]{:S(2)}) collective-permute-start(bf16[256,128]{1,0:T(8,128)(2,1)} %param.8), channel_id=1, source_target_pairs={{0,32},{32,64},{64,96},{96,128},{128,160},{160,192},{192,224},{224... | collective-permute-start | bytes 196616 | tf_op jit(solution)/shard_map/ppermute | solution.py:111
  3.1 27.1 %collective-permute-start.8 = (bf16[256,128]{1,0:T(8,128)(2,1)}, bf16[256,128]{1,0:T(8,128)(2,1)}, u32[]{:S(2)}, u32[]{:S(2)}) collective-permute-start(bf16[256,128]{1,0:T(8,128)(2,1)} %param.8), channel_id=1, source_target_pairs={{32,0},{64,32},{96,64},{128,96},{160,128},{192,160},{224,192},{256... | collective-permute-start | bytes 196616 | tf_op jit(solution)/shard_map/ppermute | solution.py:113
  7.9 53.7 %all-to-all-start = ((bf16[128,32,128]{2,0,1:T(8,128)(2,1)}), bf16[128,32,128]{2,0,1:T(8,128)(2,1)S(1)}, u32[]{:S(2)}, u32[]{:S(2)}) async-start(bf16[128,32,128]{2,0,1:T(8,128)(2,1)} %copy.27), calls=%async_computation | async-start | bytes 2097152 | tf_op jit(solution)/shard_map/all_to_all | solution.py:118
  21.4 9.8 %copy-start.10 = (bf16[256,128]{1,0:T(8,128)(2,1)}, bf16[256,128]{1,0:T(8,128)(2,1)S(1)}, u32[]{:S(2)}) copy-start(bf16[256,128]{1,0:T(8,128)(2,1)S(1)} %collective-permute-done) | copy-start | bytes 196612
  21.4 4.9 %collective-permute-start.1 = (bf16[256,128]{1,0:T(8,128)(2,1)S(1)}, bf16[256,128]{1,0:T(8,128)(2,1)S(1)}, u32[]{:S(2)}, u32[]{:S(2)}) collective-permute-start(bf16[256,128]{1,0:T(8,128)(2,1)S(1)} %collective-permute-done), channel_id=1, source_target_pairs={{0,32},{32,64},{64,96},{96,128},{128,160},{160,192},{192,224},{224... | collective-permute-start | bytes 196616 | tf_op jit(solution)/shard_map/ppermute | solution.py:111
  26.3 4.9 %collective-permute-start.2 = (bf16[256,128]{1,0:T(8,128)(2,1)S(1)}, bf16[256,128]{1,0:T(8,128)(2,1)S(1)}, u32[]{:S(2)}, u32[]{:S(2)}) collective-permute-start(bf16[256,128]{1,0:T(8,128)(2,1)S(1)} %collective-permute-done.1), channel_id=1, source_target_pairs={{0,32},{32,64},{64,96},{96,128},{128,160},{160,192},{192,224},{224... | collective-permute-start | bytes 196616 | tf_op jit(solution)/shard_map/ppermute | solution.py:111
  30.2 5.4 %collective-permute-start.9 = (bf16[256,128]{1,0:T(8,128)(2,1)}, bf16[256,128]{1,0:T(8,128)(2,1)S(1)}, u32[]{:S(2)}, u32[]{:S(2)}) collective-permute-start(bf16[256,128]{1,0:T(8,128)(2,1)} %collective-permute-done.8), channel_id=1, source_target_pairs={{32,0},{64,32},{96,64},{128,96},{160,128},{192,160},{224,192},{256... | collective-permute-start | bytes 196616 | tf_op jit(solution)/shard_map/ppermute | solution.py:113
  31.2 4.9 %collective-permute-start.3 = (bf16[256,128]{1,0:T(8,128)(2,1)S(1)}, bf16[256,128]{1,0:T(8,128)(2,1)S(1)}, u32[]{:S(2)}, u32[]{:S(2)}) collective-permute-start(bf16[256,128]{1,0:T(8,128)(2,1)S(1)} %collective-permute-done.2), channel_id=1, source_target_pairs={{0,32},{32,64},{64,96},{96,128},{128,160},{160,192},{192,224},{224... | collective-permute-start | bytes 196616 | tf_op jit(solution)/shard_map/ppermute | solution.py:111
  35.6 5.2 %collective-permute-start.10 = (bf16[256,128]{1,0:T(8,128)(2,1)S(1)}, bf16[256,128]{1,0:T(8,128)(2,1)S(1)}, u32[]{:S(2)}, u32[]{:S(2)}) collective-permute-start(bf16[256,128]{1,0:T(8,128)(2,1)S(1)} %collective-permute-done.9), channel_id=1, source_target_pairs={{32,0},{64,32},{96,64},{128,96},{160,128},{192,160},{224,192},{256... | collective-permute-start | bytes 196616 | tf_op jit(solution)/shard_map/ppermute | solution.py:113
  36.1 4.9 %collective-permute-start.4 = (bf16[256,128]{1,0:T(8,128)(2,1)S(1)}, bf16[256,128]{1,0:T(8,128)(2,1)S(1)}, u32[]{:S(2)}, u32[]{:S(2)}) collective-permute-start(bf16[256,128]{1,0:T(8,128)(2,1)S(1)} %collective-permute-done.3), channel_id=1, source_target_pairs={{0,32},{32,64},{64,96},{96,128},{128,160},{160,192},{192,224},{224... | collective-permute-start | bytes 196616 | tf_op jit(solution)/shard_map/ppermute | solution.py:111
  40.8 4.9 %collective-permute-start.11 = (bf16[256,128]{1,0:T(8,128)(2,1)S(1)}, bf16[256,128]{1,0:T(8,128)(2,1)S(1)}, u32[]{:S(2)}, u32[]{:S(2)}) collective-permute-start(bf16[256,128]{1,0:T(8,128)(2,1)S(1)} %collective-permute-done.10), channel_id=1, source_target_pairs={{32,0},{64,32},{96,64},{128,96},{160,128},{192,160},{224,192},{256... | collective-permute-start | bytes 196616 | tf_op jit(solution)/shard_map/ppermute | solution.py:113
  41.0 4.9 %collective-permute-start.5 = (bf16[256,128]{1,0:T(8,128)(2,1)S(1)}, bf16[256,128]{1,0:T(8,128)(2,1)S(1)}, u32[]{:S(2)}, u32[]{:S(2)}) collective-permute-start(bf16[256,128]{1,0:T(8,128)(2,1)S(1)} %collective-permute-done.4), channel_id=1, source_target_pairs={{0,32},{32,64},{64,96},{96,128},{128,160},{160,192},{192,224},{224... | collective-permute-start | bytes 196616 | tf_op jit(solution)/shard_map/ppermute | solution.py:111
  45.7 4.9 %collective-permute-start.12 = (bf16[256,128]{1,0:T(8,128)(2,1)S(1)}, bf16[256,128]{1,0:T(8,128)(2,1)S(1)}, u32[]{:S(2)}, u32[]{:S(2)}) collective-permute-start(bf16[256,128]{1,0:T(8,128)(2,1)S(1)} %collective-permute-done.11), channel_id=1, source_target_pairs={{32,0},{64,32},{96,64},{128,96},{160,128},{192,160},{224,192},{256... | collective-permute-start | bytes 196616 | tf_op jit(solution)/shard_map/ppermute | solution.py:113
  45.9 4.9 %collective-permute-start.6 = (bf16[256,128]{1,0:T(8,128)(2,1)S(1)}, bf16[256,128]{1,0:T(8,128)(2,1)S(1)}, u32[]{:S(2)}, u32[]{:S(2)}) collective-permute-start(bf16[256,128]{1,0:T(8,128)(2,1)S(1)} %collective-permute-done.5), channel_id=1, source_target_pairs={{0,32},{32,64},{64,96},{96,128},{128,160},{160,192},{192,224},{224... | collective-permute-start | bytes 196616 | tf_op jit(solution)/shard_map/ppermute | solution.py:111
  50.6 4.9 %collective-permute-start.13 = (bf16[256,128]{1,0:T(8,128)(2,1)S(1)}, bf16[256,128]{1,0:T(8,128)(2,1)S(1)}, u32[]{:S(2)}, u32[]{:S(2)}) collective-permute-start(bf16[256,128]{1,0:T(8,128)(2,1)S(1)} %collective-permute-done.12), channel_id=1, source_target_pairs={{32,0},{64,32},{96,64},{128,96},{160,128},{192,160},{224,192},{256... | collective-permute-start | bytes 196616 | tf_op jit(solution)/shard_map/ppermute | solution.py:113
  50.8 4.9 %collective-permute-start.7 = (bf16[256,128]{1,0:T(8,128)(2,1)S(1)}, bf16[256,128]{1,0:T(8,128)(2,1)S(1)}, u32[]{:S(2)}, u32[]{:S(2)}) collective-permute-start(bf16[256,128]{1,0:T(8,128)(2,1)S(1)} %collective-permute-done.6), channel_id=1, source_target_pairs={{0,32},{32,64},{64,96},{96,128},{128,160},{160,192},{192,224},{224... | collective-permute-start | bytes 196616 | tf_op jit(solution)/shard_map/ppermute | solution.py:111
  55.5 4.9 %collective-permute-start.14 = (bf16[256,128]{1,0:T(8,128)(2,1)S(1)}, bf16[256,128]{1,0:T(8,128)(2,1)S(1)}, u32[]{:S(2)}, u32[]{:S(2)}) collective-permute-start(bf16[256,128]{1,0:T(8,128)(2,1)S(1)} %collective-permute-done.13), channel_id=1, source_target_pairs={{32,0},{64,32},{96,64},{128,96},{160,128},{192,160},{224,192},{256... | collective-permute-start | bytes 196616 | tf_op jit(solution)/shard_map/ppermute | solution.py:113
  74.9 4.5 %copy-start = (f32[2,128,64,128]{3,2,1,0:T(8,128)}, f32[2,128,64,128]{3,2,1,0:T(8,128)S(1)}, u32[]{:S(2)}) copy-start(f32[2,128,64,128]{3,2,1,0:T(8,128)S(1)} %fusion.12) | copy-start | bytes 25165828
  86.1 4.6 %copy-start.1 = (f32[2,128,64,128]{3,2,1,0:T(8,128)S(1)}, f32[2,128,64,128]{3,2,1,0:T(8,128)}, u32[]{:S(2)}) copy-start(f32[2,128,64,128]{3,2,1,0:T(8,128)} %copy-done) | copy-start | bytes 25165828
  105.9 6.2 %slice-start = ((f32[128,8192]{1,0:T(8,128)}), f32[64,8192]{1,0:T(8,128)S(1)}, s32[]{:S(2)}) async-start(f32[128,8192]{1,0:T(8,128)} %copy-done.2), calls=%async_computation.2 | async-start | bytes 4194304 | tf_op jit(solution)/shard_map/slice | solution.py:122
  108.4 15.8 %copy-start.11 = (f32[128]{0:T(128)S(1)}, f32[128]{0:T(128)}, u32[]{:S(2)}) copy-start(f32[128]{0:T(128)} %param.9) | copy-start | bytes 1540
  108.4 15.8 %collective-permute-start.15 = (bf16[4096,128]{1,0:T(8,128)(2,1)}, bf16[4096,128]{1,0:T(8,128)(2,1)}, u32[]{:S(2)}, u32[]{:S(2)}) collective-permute-start(bf16[4096,128]{1,0:T(8,128)(2,1)} %convert_element_type.128), channel_id=1, source_target_pairs={{0,32},{32,64},{64,96},{96,128},{128,160},{160,192},{192,224},{224... | collective-permute-start | bytes 3145736 | tf_op jit(solution)/shard_map/ppermute | solution.py:20
  113.7 22.9 %copy-start.3 = (bf16[128,4096]{1,0:T(8,128)(2,1)S(1)}, bf16[128,4096]{1,0:T(8,128)(2,1)}, u32[]{:S(2)}) copy-start(bf16[128,4096]{1,0:T(8,128)(2,1)} %param.5) | copy-start | bytes 3145732
  127.4 35.7 %all-to-all-start.1 = ((bf16[32,128,128]{2,1,0:T(8,128)(2,1)}), bf16[32,128,128]{2,1,0:T(8,128)(2,1)S(1)}, u32[]{:S(2)}, u32[]{:S(2)}) async-start(bf16[32,128,128]{2,1,0:T(8,128)(2,1)} %bitcast.42), calls=%async_computation.1 | async-start | bytes 2097152 | tf_op jit(solution)/shard_map/all_to_all | solution.py:129
  (7 other events, 14.9 us)
